TPU v7x, 32 devices: a whole 2x2x4 slice. The times are simulated.
32 devices in a mesh: space: 8 (over z, y), chan: 4 (over x, core).
Axes of the slice: x: 2, y: 2, z: 4, core: 2. Of those that a mesh axis runs over, the one named last changes fastest.
Arguments:
- inputs: bfloat16 [128, 16, 16, 128], P('chan', 'space'), may hold values from -6 to 6
- weight: bfloat16 [128, 27, 128], P(None, None, 'chan'), may hold values from -0.109375 to 0.109375
- cotangent: bfloat16 [128, 16, 16, 128], P('chan', 'space'), may hold values from -6 to 6
Outputs:
- output: bfloat16 [128, 16, 16, 128], P('chan', 'space')
- grad_inputs: bfloat16 [128, 16, 16, 128], P('chan', 'space')
- grad_weight: float32 [128, 27, 128], P('space', None, 'chan')
All inputs are finite; a program needn't handle non-finite values.
Results may differ from a plain program's by a relative error of at most 0.0085.
Values may be sent and summed in bfloat16 or wider, within the bound.
A program may use at most 64 MiB of HBM per device.

v0:
```python
import jax
import jax.numpy as jnp
from jax import lax
from jax.sharding import PartitionSpec as P


def padded(cells, sides, width):
    for axis, dim in sides:
        count = lax.axis_size(axis)
        head = lax.slice_in_dim(cells, 0, width, axis=dim)
        tail = lax.slice_in_dim(cells, cells.shape[dim] - width, cells.shape[dim], axis=dim)
        cells = jnp.concatenate(
            [
                lax.ppermute(tail, axis, [(i, (i + 1) % count) for i in range(count)]),
                cells,
                lax.ppermute(head, axis, [((i + 1) % count, i) for i in range(count)]),
            ],
            axis=dim,
        )
    return cells


def tap_offsets():
    return [
        (shift_d, shift_h, shift_w)
        for shift_d in (-1, 0, 1)
        for shift_h in (-1, 0, 1)
        for shift_w in (-1, 0, 1)
    ]


def per_device(inputs, weight, cotangent):
    depth_local = inputs.shape[1]
    moved_inputs, moved_cot = (
        lax.all_to_all(inputs, "chan", split_axis=2, concat_axis=0, tiled=True),
        lax.all_to_all(cotangent, "chan", split_axis=2, concat_axis=0, tiled=True),
    )
    rows_local = moved_inputs.shape[2]
    extended = padded(moved_inputs, (("space", 1), ("chan", 2)), 1)
    filters = lax.all_gather(weight, "chan", axis=2, tiled=True)
    pre_act = jnp.zeros(moved_inputs.shape, jnp.float32)
    for index_tap, (shift_d, shift_h, shift_w) in enumerate(tap_offsets()):
        piece = extended[
            :, 1 + shift_d : 1 + shift_d + depth_local, 1 + shift_h : 1 + shift_h + rows_local
        ]
        piece = jnp.roll(piece, -shift_w, axis=3)
        pre_act = pre_act + jnp.einsum(
            "idhw,io->odhw", piece, filters[:, index_tap, :], preferred_element_type=jnp.float32
        )
    out_local = jnp.maximum(pre_act, 0.0).astype(jnp.bfloat16)
    grad_pre = jnp.where(pre_act > 0, moved_cot.astype(jnp.float32), 0.0).astype(jnp.bfloat16)
    output = lax.all_to_all(out_local, "chan", split_axis=0, concat_axis=2, tiled=True)
    grad_ext = padded(grad_pre, (("space", 1), ("chan", 2)), 1)
    grad_sum = jnp.zeros(moved_inputs.shape, jnp.float32)
    for index_tap, (shift_d, shift_h, shift_w) in enumerate(tap_offsets()):
        piece = grad_ext[
            :, 1 - shift_d : 1 - shift_d + depth_local, 1 - shift_h : 1 - shift_h + rows_local
        ]
        piece = jnp.roll(piece, shift_w, axis=3)
        grad_sum = grad_sum + jnp.einsum(
            "odhw,io->idhw", piece, filters[:, index_tap, :], preferred_element_type=jnp.float32
        )
    grad_inputs = lax.all_to_all(
        grad_sum.astype(jnp.bfloat16), "chan", split_axis=0, concat_axis=2, tiled=True
    )
    tap_list = []
    for index_tap, (shift_d, shift_h, shift_w) in enumerate(tap_offsets()):
        piece = extended[
            :, 1 + shift_d : 1 + shift_d + depth_local, 1 + shift_h : 1 + shift_h + rows_local
        ]
        piece = jnp.roll(piece, -shift_w, axis=3)
        tap_list.append(
            jnp.einsum("idhw,odhw->io", piece, grad_pre, preferred_element_type=jnp.float32)
        )
    partial_sum = lax.psum_scatter(
        jnp.stack(tap_list, axis=1), "space", scatter_dimension=0, tiled=True
    )
    grad_weight = lax.psum_scatter(partial_sum, "chan", scatter_dimension=2, tiled=True)
    return (output, grad_inputs, grad_weight)


def solution(mesh):
    in_specs = (
        P("chan", "space", None, None),
        P(None, None, "chan"),
        P("chan", "space", None, None),
    )
    out_specs = (
        P("chan", "space", None, None),
        P("chan", "space", None, None),
        P("space", None, "chan"),
    )
    return jax.shard_map(
        per_device, mesh=mesh, in_specs=in_specs, out_specs=out_specs, check_vma=False
    )
```

profile of v0, /device:TPU:0, one launch (start us, length us, event | category | flops | bytes accessed | tf_op | source)
XLA Modules:
  0.0 178.1 jit_solution(6545639323441884272)
XLA Ops:
  7.2 1.8 %copy.210 = bf16[32,2,16,128]{3,0,1,2:T(8,128)(2,1)} copy(bf16[32,2,16,128]{3,2,1,0:T(8,128)(2,1)} %param.3) | data formatting | bytes 524288 | tf_op args[0]
  9.0 4.2 %all-to-all-start = ((bf16[32,2,16,128]{3,0,1,2:T(8,128)(2,1)}), bf16[32,2,16,128]{3,0,1,2:T(8,128)(2,1)S(1)}, u32[]{:S(2)}, u32[]{:S(2)}) async-start(bf16[32,2,16,128]{3,0,1,2:T(8,128)(2,1)} %copy.210), calls=%async_computation | async-start | bytes 524288 | tf_op jit(solution)/shard_map/all_to_all | solution.py:35
  13.2 1.8 copy.253
  14.9 9.9 %all_gather.3 = bf16[128,27,128]{0,2,1:T(8,128)(2,1)S(1)} all-gather(bf16[128,27,32]{0,2,1:T(8,128)(2,1)S(1)} %copy-done.2), channel_id=1, replica_groups=mesh['space'=8,'chan'=4] {'chan'}, dimensions={2}, use_global_device_ids=true | all-gather | bytes 1105920 | tf_op jit(solution)/shard_map/all_gather | solution.py:40
  24.9 3.4 %all-to-all-start.2 = ((bf16[32,2,16,128]{3,0,1,2:T(8,128)(2,1)}), bf16[32,2,16,128]{3,0,1,2:T(8,128)(2,1)S(1)}, u32[]{:S(2)}, u32[]{:S(2)}) async-start(bf16[32,2,16,128]{3,0,1,2:T(8,128)(2,1)} %copy.253), calls=%async_computation.2 | async-start | bytes 524288 | tf_op jit(solution)/shard_map/all_to_all | solution.py:36
  28.6 2.2 %collective-permute-start = (bf16[128,1,4,128]{0,3,2,1:T(8,128)(2,1)S(1)}, bf16[128,1,4,128]{0,3,2,1:T(8,128)(2,1)S(1)}, u32[]{:S(2)}, u32[]{:S(2)}) collective-permute-start(bf16[128,1,4,128]{0,3,2,1:T(8,128)(2,1)S(1)} %get-tuple-element.88), channel_id=1, source_target_pairs={{0,4},{4,8},{8,12},{12,16},{16,20},{20,24},{24,28},{28,0},{1,5},{5... | collective-permute-start | bytes 393224 | tf_op jit(solution)/shard_map/ppermute | solution.py:14
  30.7 3.1 %collective-permute-start.1 = (bf16[128,1,4,128]{0,3,2,1:T(8,128)(2,1)S(1)}, bf16[128,1,4,128]{0,3,2,1:T(8,128)(2,1)S(1)}, u32[]{:S(2)}, u32[]{:S(2)}) collective-permute-start(bf16[128,1,4,128]{0,3,2,1:T(8,128)(2,1)S(1)} %get-tuple-element.89), channel_id=1, source_target_pairs={{4,0},{8,4},{12,8},{16,12},{20,16},{24,20},{28,24},{0,28},{5,1},{9... | collective-permute-start | bytes 393224 | tf_op jit(solution)/shard_map/ppermute | solution.py:16
  34.7 3.2 %collective-permute-done = bf16[128,1,4,128]{0,3,2,1:T(8,128)(2,1)S(1)} collective-permute-done((bf16[128,1,4,128]{0,3,2,1:T(8,128)(2,1)S(1)}, bf16[128,1,4,128]{0,3,2,1:T(8,128)(2,1)S(1)}, u32[]{:S(2)}, u32[]{:S(2)}) %collective-permute-start) | collective-permute-done | bytes 131104 | tf_op jit(solution)/shard_map/ppermute | solution.py:14
  38.0 1.1 collective-permute-done.1
  39.2 1.7 collective-permute-start.3
  42.8 0.8 collective-permute-done.2
  43.6 0.6 collective-permute-done.3
  44.3 0.8 fusion.233
  50.2 0.6 select_convert_fusion
  50.9 0.9 fusion.73
  51.8 0.9 fusion.54
  52.7 0.9 fusion.72
  53.6 0.9 fusion.71
  54.5 0.9 fusion.53
  55.4 0.9 fusion.70
  56.3 0.9 fusion.69
  57.2 0.9 fusion.52
  58.1 0.9 fusion.68
  59.0 0.9 fusion.67
  59.9 0.9 fusion.51
  60.8 0.9 fusion.66
  61.7 0.9 fusion.65
  62.6 0.8 fusion.55
  63.4 0.9 fusion.64
  64.3 0.9 fusion.63
  65.2 0.9 fusion.50
  66.1 0.9 fusion.62
  67.0 0.9 fusion.61
  67.9 0.9 fusion.49
  68.7 0.9 fusion.60
  69.6 0.9 fusion.59
  70.5 0.9 fusion.48
  71.4 0.9 fusion.58
  72.3 0.9 fusion.57
  73.5 4.5 %collective-permute-start.5 = (bf16[128,1,4,128]{0,3,2,1:T(8,128)(2,1)S(1)}, bf16[128,1,4,128]{0,3,2,1:T(8,128)(2,1)S(1)}, u32[]{:S(2)}, u32[]{:S(2)}) collective-permute-start(bf16[128,1,4,128]{0,3,2,1:T(8,128)(2,1)S(1)} %get-tuple-element.78), channel_id=1, source_target_pairs={{4,0},{8,4},{12,8},{16,12},{20,16},{24,20},{28,24},{0,28},{5,1},{9... | collective-permute-start | bytes 393224 | tf_op jit(solution)/shard_map/ppermute | solution.py:16
  77.9 0.9 fusion.47
  78.8 0.9 fusion.56
  79.8 0.9 copy.250
  80.7 4.0 %all-to-all-start.1 = ((bf16[128,2,4,128]{3,2,1,0:T(4,128)(2,1)}), bf16[128,2,4,128]{3,2,1,0:T(4,128)(2,1)}, u32[]{:S(2)}, u32[]{:S(2)}) async-start(bf16[128,2,4,128]{3,2,1,0:T(4,128)(2,1)} %copy.250), calls=%async_computation.1 | async-start | bytes 524288 | tf_op jit(solution)/shard_map/all_to_all | solution.py:52
  84.8 1.9 %collective-permute-start.6 = (bf16[128,4,1,128]{0,3,2,1:T(8,128)(2,1)S(1)}, bf16[128,4,1,128]{0,3,2,1:T(8,128)(2,1)S(1)}, u32[]{:S(2)}, u32[]{:S(2)}) collective-permute-start(bf16[128,4,1,128]{0,3,2,1:T(8,128)(2,1)S(1)} %get-tuple-element.47), channel_id=1, source_target_pairs={{1,0},{2,1},{3,2},{0,3},{5,4},{6,5},{7,6},{4,7},{9,8},{10,9},{11,1... | collective-permute-start | bytes 393224 | tf_op jit(solution)/shard_map/ppermute | solution.py:16
  87.9 1.0 convolution_bitcast_fusion.9
  88.9 2.6 %collective-permute-done.6 = bf16[128,4,1,128]{0,3,2,1:T(8,128)(2,1)S(1)} collective-permute-done((bf16[128,4,1,128]{0,3,2,1:T(8,128)(2,1)S(1)}, bf16[128,4,1,128]{0,3,2,1:T(8,128)(2,1)S(1)}, u32[]{:S(2)}, u32[]{:S(2)}) %collective-permute-start.6) | collective-permute-done | bytes 131104 | tf_op jit(solution)/shard_map/ppermute | solution.py:16
  91.5 1.5 collective-permute-done.7
  94.9 1.0 convolution_bitcast_fusion
  97.4 1.0 convolution_bitcast_fusion.7
  100.0 1.1 fusion.45
  101.0 44.5 %reduce-scatter.5.cloned.1.call-done = f32[16,27,128]{2,0,1:T(8,128)} async-done(((f32[128,27,128]{2,0,1:T(8,128)}), f32[16,27,128]{2,0,1:T(8,128)}) %reduce-scatter.5.cloned.1.call-update) | async-done | bytes 221200 | tf_op jit(solution)/shard_map/reduce_scatter | solution.py:75
  145.6 2.6 %copy.425 = f32[16,27,128]{0,1,2:T(8,128)S(1)} copy(f32[16,27,128]{2,0,1:T(8,128)} %reduce-scatter.5.cloned.1.call-done) | data formatting | bytes 442368
  148.2 2.0 %reshape.68 = f32[128,432]{1,0:T(8,128)} reshape(f32[128,27,16]{2,1,0:T(8,128)S(1)} %bitcast.667) | data formatting | bytes 442368
  150.2 1.6 fusion.46
  151.8 0.9 copy.257
  152.7 3.4 %all-to-all-start.3 = ((bf16[128,2,4,128]{3,2,1,0:T(4,128)(2,1)}), bf16[128,2,4,128]{3,2,1,0:T(4,128)(2,1)S(1)}, u32[]{:S(2)}, u32[]{:S(2)}) async-start(bf16[128,2,4,128]{3,2,1,0:T(4,128)(2,1)} %copy.257), calls=%async_computation.3 | async-start | bytes 524288 | tf_op jit(solution)/shard_map/all_to_all | solution.py:63
  156.1 1.0 copy.251
  157.2 0.8 copy.314
  158.0 4.2 %all-to-all-done.3 = bf16[128,2,4,128]{3,2,1,0:T(4,128)(2,1)S(1)} async-done(((bf16[128,2,4,128]{3,2,1,0:T(4,128)(2,1)}), bf16[128,2,4,128]{3,2,1,0:T(4,128)(2,1)S(1)}, u32[]{:S(2)}, u32[]{:S(2)}) %all-to-all-start.3) | async-done | bytes 262176 | tf_op jit(solution)/shard_map/all_to_all | solution.py:63
  162.2 0.8 copy.315
  163.0 6.2 %reduce-scatter.7.cloned.1.call-done = f32[32,432]{1,0:T(8,128)} async-done(((f32[128,432]{1,0:T(8,128)}), f32[32,432]{1,0:T(8,128)}) %reduce-scatter.7.cloned.1.call-update) | async-done | bytes 55312
  169.3 1.1 reshape.69
  170.3 1.0 copy.426
  (90 shorter events, 14.5 us)
Async XLA Ops:
  7.2 7.8 %copy-start.2 = (bf16[128,27,32]{0,2,1:T(8,128)(2,1)S(1)}, bf16[128,27,32]{0,2,1:T(8,128)(2,1)}, u32[]{:S(2)}) copy-start(bf16[128,27,32]{0,2,1:T(8,128)(2,1)} %param.4) | copy-start | bytes 663556
  9.0 15.9 %all-to-all-start = ((bf16[32,2,16,128]{3,0,1,2:T(8,128)(2,1)}), bf16[32,2,16,128]{3,0,1,2:T(8,128)(2,1)S(1)}, u32[]{:S(2)}, u32[]{:S(2)}) async-start(bf16[32,2,16,128]{3,0,1,2:T(8,128)(2,1)} %copy.210), calls=%async_computation | async-start | bytes 524288 | tf_op jit(solution)/shard_map/all_to_all | solution.py:35
  24.9 75.1 %copy-start = (bf16[128,27,128]{0,2,1:T(8,128)(2,1)}, bf16[128,27,128]{0,2,1:T(8,128)(2,1)S(1)}, u32[]{:S(2)}) copy-start(bf16[128,27,128]{0,2,1:T(8,128)(2,1)S(1)} %all_gather.3) | copy-start | bytes 2654212
  24.9 9.4 %all-to-all-start.2 = ((bf16[32,2,16,128]{3,0,1,2:T(8,128)(2,1)}), bf16[32,2,16,128]{3,0,1,2:T(8,128)(2,1)S(1)}, u32[]{:S(2)}, u32[]{:S(2)}) async-start(bf16[32,2,16,128]{3,0,1,2:T(8,128)(2,1)} %copy.253), calls=%async_computation.2 | async-start | bytes 524288 | tf_op jit(solution)/shard_map/all_to_all | solution.py:36
  28.3 117.3 %reduce-scatter.5.cloned.1.call-start = ((), (), s32[]{:S(2)}) async-start(), calls=%async_computation.6 | async-start | bytes 1990656 | tf_op jit(solution)/shard_map/reduce_scatter | solution.py:75
  28.6 9.4 %collective-permute-start = (bf16[128,1,4,128]{0,3,2,1:T(8,128)(2,1)S(1)}, bf16[128,1,4,128]{0,3,2,1:T(8,128)(2,1)S(1)}, u32[]{:S(2)}, u32[]{:S(2)}) collective-permute-start(bf16[128,1,4,128]{0,3,2,1:T(8,128)(2,1)S(1)} %get-tuple-element.88), channel_id=1, source_target_pairs={{0,4},{4,8},{8,12},{12,16},{16,20},{20,24},{24,28},{28,0},{1,5},{5... | collective-permute-start | bytes 393224 | tf_op jit(solution)/shard_map/ppermute | solution.py:14
  30.7 8.4 %collective-permute-start.1 = (bf16[128,1,4,128]{0,3,2,1:T(8,128)(2,1)S(1)}, bf16[128,1,4,128]{0,3,2,1:T(8,128)(2,1)S(1)}, u32[]{:S(2)}, u32[]{:S(2)}) collective-permute-start(bf16[128,1,4,128]{0,3,2,1:T(8,128)(2,1)S(1)} %get-tuple-element.89), channel_id=1, source_target_pairs={{4,0},{8,4},{12,8},{16,12},{20,16},{24,20},{28,24},{0,28},{5,1},{9... | collective-permute-start | bytes 393224 | tf_op jit(solution)/shard_map/ppermute | solution.py:16
  39.1 4.4 %collective-permute-start.2 = (bf16[128,4,1,128]{0,3,2,1:T(8,128)(2,1)S(1)}, bf16[128,4,1,128]{0,3,2,1:T(8,128)(2,1)S(1)}, u32[]{:S(2)}, u32[]{:S(2)}) collective-permute-start(bf16[128,4,1,128]{0,3,2,1:T(8,128)(2,1)S(1)} %get-tuple-element.53), channel_id=1, source_target_pairs={{0,1},{1,2},{2,3},{3,0},{4,5},{5,6},{6,7},{7,4},{8,9},{9,10},{10,1... | collective-permute-start | bytes 393224 | tf_op jit(solution)/shard_map/ppermute | solution.py:14
  39.2 5.0 %collective-permute-start.3 = (bf16[128,4,1,128]{0,3,2,1:T(8,128)(2,1)S(1)}, bf16[128,4,1,128]{0,3,2,1:T(8,128)(2,1)S(1)}, u32[]{:S(2)}, u32[]{:S(2)}) collective-permute-start(bf16[128,4,1,128]{0,3,2,1:T(8,128)(2,1)S(1)} %get-tuple-element.54), channel_id=1, source_target_pairs={{1,0},{2,1},{3,2},{0,3},{5,4},{6,5},{7,6},{4,7},{9,8},{10,9},{11,1... | collective-permute-start | bytes 393224 | tf_op jit(solution)/shard_map/ppermute | solution.py:16
  73.2 11.5 %collective-permute-start.4 = (bf16[128,1,4,128]{0,3,2,1:T(8,128)(2,1)S(1)}, bf16[128,1,4,128]{0,3,2,1:T(8,128)(2,1)S(1)}, u32[]{:S(2)}, u32[]{:S(2)}) collective-permute-start(bf16[128,1,4,128]{0,3,2,1:T(8,128)(2,1)S(1)} %get-tuple-element.77), channel_id=1, source_target_pairs={{0,4},{4,8},{8,12},{12,16},{16,20},{20,24},{24,28},{28,0},{1,5},{5... | collective-permute-start | bytes 393224 | tf_op jit(solution)/shard_map/ppermute | solution.py:14
  73.5 11.3 %collective-permute-start.5 = (bf16[128,1,4,128]{0,3,2,1:T(8,128)(2,1)S(1)}, bf16[128,1,4,128]{0,3,2,1:T(8,128)(2,1)S(1)}, u32[]{:S(2)}, u32[]{:S(2)}) collective-permute-start(bf16[128,1,4,128]{0,3,2,1:T(8,128)(2,1)S(1)} %get-tuple-element.78), channel_id=1, source_target_pairs={{4,0},{8,4},{12,8},{16,12},{20,16},{24,20},{28,24},{0,28},{5,1},{9... | collective-permute-start | bytes 393224 | tf_op jit(solution)/shard_map/ppermute | solution.py:16
  80.7 72.1 %all-to-all-start.1 = ((bf16[128,2,4,128]{3,2,1,0:T(4,128)(2,1)}), bf16[128,2,4,128]{3,2,1,0:T(4,128)(2,1)}, u32[]{:S(2)}, u32[]{:S(2)}) async-start(bf16[128,2,4,128]{3,2,1,0:T(4,128)(2,1)} %copy.250), calls=%async_computation.1 | async-start | bytes 524288 | tf_op jit(solution)/shard_map/all_to_all | solution.py:52
  84.7 84.6 %reduce-scatter.7.cloned.1.call-start = ((), (), s32[]{:S(2)}) async-start(), calls=%async_computation.7 | async-start | bytes 327680
  84.8 6.7 %collective-permute-start.6 = (bf16[128,4,1,128]{0,3,2,1:T(8,128)(2,1)S(1)}, bf16[128,4,1,128]{0,3,2,1:T(8,128)(2,1)S(1)}, u32[]{:S(2)}, u32[]{:S(2)}) collective-permute-start(bf16[128,4,1,128]{0,3,2,1:T(8,128)(2,1)S(1)} %get-tuple-element.47), channel_id=1, source_target_pairs={{1,0},{2,1},{3,2},{0,3},{5,4},{6,5},{7,6},{4,7},{9,8},{10,9},{11,1... | collective-permute-start | bytes 393224 | tf_op jit(solution)/shard_map/ppermute | solution.py:16
  86.7 6.3 %collective-permute-start.7 = (bf16[128,4,1,128]{0,3,2,1:T(8,128)(2,1)S(1)}, bf16[128,4,1,128]{0,3,2,1:T(8,128)(2,1)S(1)}, u32[]{:S(2)}, u32[]{:S(2)}) collective-permute-start(bf16[128,4,1,128]{0,3,2,1:T(8,128)(2,1)S(1)} %get-tuple-element.48), channel_id=1, source_target_pairs={{0,1},{1,2},{2,3},{3,0},{4,5},{5,6},{6,7},{7,4},{8,9},{9,10},{10,1... | collective-permute-start | bytes 393224 | tf_op jit(solution)/shard_map/ppermute | solution.py:14
  148.2 2.0 %copy-start.1 = (f32[128,2,4,128]{0,3,2,1:T(8,128)S(1)}, f32[128,2,4,128]{0,3,2,1:T(8,128)}, u32[]{:S(2)}) copy-start(f32[128,2,4,128]{0,3,2,1:T(8,128)} %convolution_bitcast_fusion.7) | copy-start | bytes 1572868
  152.7 9.4 %all-to-all-start.3 = ((bf16[128,2,4,128]{3,2,1,0:T(4,128)(2,1)}), bf16[128,2,4,128]{3,2,1,0:T(4,128)(2,1)S(1)}, u32[]{:S(2)}, u32[]{:S(2)}) async-start(bf16[128,2,4,128]{3,2,1,0:T(4,128)(2,1)} %copy.257), calls=%async_computation.3 | async-start | bytes 524288 | tf_op jit(solution)/shard_map/all_to_all | solution.py:63
Sparse Core Ops, SparseCore 0:
  79.9 65.6 reduce-scatter.4
  150.3 18.9 reduce-scatter.6
where the time goes:
time: 179 us; the launch traced here: 178 us
  waiting for transfers between devices  65.3 us (36%)
  matrix products  41.6 us (23%)
  starting transfers between devices  28.9 us (16%)
  local copies, waits for them, and re-layouts  16.5 us (9%)
  between operations  14.6 us (8%)
  blocking collectives  9.91 us (6%)
    reduce_scatter x1, waiting for transfers between devices, per_device(): lax.psum_scatter(jnp.stack(tap_list, axis=1), 'space', scatter_dimension=...  44.5 us
    dot_general x27, matrix products, per_device(): jnp.einsum('idhw,odhw->io', piece, grad_pre, preferred_element_type=jnp.f...  24.1 us
    unnamed x14, local copies, waits for them, and re-layouts  11.8 us
    ppermute x4, starting transfers between devices, padded(): lax.ppermute(head, axis, [((i + 1) % count, i) for i in range(count)])  11.2 us
    dot_general x27, matrix products, per_device(): jnp.einsum('odhw,io->idhw', piece, filters[:, index_tap, :], preferred_el...  10.6 us
    all_gather x1, blocking collectives, per_device(): filters = lax.all_gather(weight, 'chan', axis=2, tiled=True)  9.91 us
    dot_general x26, matrix products, per_device(): jnp.einsum('idhw,io->odhw', piece, filters[:, index_tap, :], preferred_el...  6.59 us
    unnamed x3, waiting for transfers between devices  6.28 us
  transfers between devices with their start and end apart: 14, of which 10 were waited for; matrix products, arithmetic and copies ran while one was open for 15% of the time, Pallas kernels for 0%

commit v1 on v0

--- a/solution.py
+++ b/solution.py
@@ -1,6 +1,10 @@
+import functools
+
 import jax
 import jax.numpy as jnp
 from jax import lax
+from jax.experimental import pallas as pl
+from jax.experimental.pallas import tpu as pltpu
 from jax.sharding import PartitionSpec as P
 
 
@@ -79,6 +83,245 @@
     return (output, grad_inputs, grad_weight)
 
 
+MESH = pl.DeviceIdType.MESH
+
+
+def stencil(filters, cells, total):
+    rows = cells.shape[0]
+    depth = cells.shape[1] * cells.shape[2] * cells.shape[3]
+    total[...] = jnp.zeros_like(total)
+
+    @pl.loop(0, rows // 2)
+    def _(pair):
+        right = jnp.concatenate(
+            [cells[2 * pair].reshape(depth, 128), cells[2 * pair + 1].reshape(depth, 128)], axis=1
+        )
+        terms = jnp.dot(filters(), right, preferred_element_type=jnp.float32)
+        for half in range(2):
+            part = terms[:, 128 * half : 128 * half + 128].reshape(2, 9, 32, 128)
+            for b in range(3):
+                one = [part[:, 3 * b + c].reshape(64, 128) for c in range(3)]
+                row = lax.rem(2 * pair + half + rows + 1 - b, rows)
+                total[row] += one[1] + pltpu.roll(one[0], 1, 1) + pltpu.roll(one[2], 127, 1)
+
+
+def kernel(
+    spaces, x_ref, cot_ref, wf_ref, wg_ref, out_ref, gi_ref, gw_ref,
+    xg, gp, wf, wg, cot, rolled, total, parts, other, sums, landed, part_out,
+    send, recv, local,
+):
+    s, c = lax.axis_index("space"), lax.axis_index("chan")
+    x, k = c // 2, lax.rem(c, 2)
+    chan = [c, 2 * x + 1 - k, lax.rem(c + 2, 4), 2 * (1 - x) + 1 - k]
+    up, down = lax.rem(s + 1, spaces), lax.rem(s + spaces - 1, spaces)
+
+    barrier = pltpu.get_barrier_semaphore()
+    greeted = [(s, other_c) for other_c in chan[1:]]
+    greeted += [(side, other_c) for side in (up, down) for other_c in range(4)]
+    greeted += [(lax.rem(s + step, spaces), c) for step in range(2, spaces - 1)]
+    for device in greeted:
+        pl.semaphore_signal(barrier, inc=1, device_id=device, device_id_type=MESH)
+    pl.semaphore_wait(barrier, len(greeted))
+
+    def start(src, dst, out_sem, in_sem, device):
+        copy = pltpu.make_async_remote_copy(
+            src_ref=src, dst_ref=dst, send_sem=send.at[out_sem], recv_sem=recv.at[in_sem],
+            device_id=device, device_id_type=MESH,
+        )
+        copy.start()
+        return copy
+
+    def wait_in(dst, in_sem):
+        pltpu.make_async_copy(dst, dst, recv.at[in_sem]).wait()
+
+    sent = []
+    keep = [
+        pltpu.make_async_copy(x_ref, xg.at[:, c, pl.ds(1 - k, 2)], local.at[0]),
+        pltpu.make_async_copy(cot_ref.at[:, k], cot.at[:, k], local.at[1]),
+        pltpu.make_async_copy(wf_ref, wf.at[k], local.at[2]),
+        pltpu.make_async_copy(wg_ref.at[x], wg.at[c], local.at[3]),
+    ]
+    for copy in keep:
+        copy.start()
+    for j in (2, 3, 1):
+        core = k if j == 2 else 1 - k
+        sent.append(start(x_ref, xg.at[:, c, pl.ds(1 - core, 2)], j - 1, j - 1, (s, chan[j])))
+    for plane, side in ((0, down), (1, up)):
+        for to_x in range(2):
+            sent.append(
+                start(
+                    x_ref.at[:, plane], xg.at[:, c, 2 * (1 - plane)],
+                    3 + 2 * plane + to_x, 3 + c, (side, 2 * to_x + 1 - plane),
+                )
+            )
+    sent.append(start(wf_ref, wf.at[k], 7, 7, (s, chan[1])))
+    sent.append(start(cot_ref.at[:, 1 - k], cot.at[:, k], 8, 8, (s, chan[1])))
+    for j in (2, 3, 1):
+        sent.append(start(wg_ref.at[chan[j] // 2], wg.at[c], 8 + j, 8 + j, (s, chan[j])))
+
+    zero = jnp.zeros((4, 32, 128), jnp.bfloat16)
+
+    @pl.loop(0, xg.shape[0])
+    def _(h):
+        xg[h, :, 3] = zero
+        gp[h, :, 3] = zero
+        rolled[h, :, 3] = zero[:2]
+
+    for copy in keep:
+        copy.wait()
+    for j in (1, 2, 3):
+        wait_in(xg.at[:, chan[j], pl.ds(1 - k, 2)], j - 1)
+    for from_c in range(4):
+        wait_in(xg.at[:, from_c, 2 * k], 3 + from_c)
+    wait_in(wf.at[1 - k], 7)
+    stencil(lambda: wf[...].reshape(576, 512), xg, total)
+    wait_in(cot.at[:, 1 - k], 8)
+
+    @pl.loop(0, xg.shape[0])
+    def _(h):
+        pre = total[h].reshape(2, 32, 128)
+        out = jnp.maximum(pre, 0.0).astype(jnp.bfloat16)
+        part_out[h] = out
+        grad = jnp.where(pre > 0, cot[h].astype(jnp.float32), 0.0)
+        gp[h, pl.ds(2 * x, 2), 1] = grad.astype(jnp.bfloat16)
+        flat = grad.reshape(64, 128)
+        rolled[h, :, 0] = pltpu.roll(flat, 127, 1).reshape(2, 32, 128).astype(jnp.bfloat16)
+        rolled[h, :, 1] = grad.astype(jnp.bfloat16)
+        rolled[h, :, 2] = pltpu.roll(flat, 1, 1).reshape(2, 32, 128).astype(jnp.bfloat16)
+
+    mine = gp.at[:, pl.ds(2 * x, 2), 1]
+
+    def place(slot):
+        return gp.at[:, pl.ds(2 * x, 2), slot]
+
+    side = lax.rem(s + spaces + 2 * k - 1, spaces)
+    sent.append(start(mine, place(1), 13, 13, (s, chan[2])))
+    sent.append(start(mine, place(2 * k), 14, 14, (s, chan[3])))
+    for to_x in range(2):
+        sent.append(start(mine, place(2 * (1 - k)), 15 + to_x, 15 + x, (side, 2 * to_x + 1 - k)))
+    sent.append(start(mine, place(2 * k), 12, 12, (s, chan[1])))
+    sent.append(start(part_out.at[:, 1 - k], out_ref.at[:, k], 17, 17, (s, chan[1])))
+    copy_out = pltpu.make_async_copy(part_out.at[:, k], out_ref.at[:, k], local.at[0])
+    copy_out.start()
+
+    rows = xg.shape[0]
+
+    @pl.loop(0, 3)
+    def _(b):
+        left = jnp.concatenate(
+            [xg[lax.rem(h + rows + b - 1, rows)].reshape(512, 128) for h in range(rows)], axis=1
+        )
+        right = jnp.concatenate([rolled[h].reshape(256, 128) for h in range(rows)], axis=1)
+        got = lax.dot_general(
+            left, right, (((1,), (1,)), ((), ())), preferred_element_type=jnp.float32
+        ).astype(jnp.bfloat16)
+        for half in range(2):
+            parts[half, b] = got[:, 128 * half : 128 * half + 128].reshape(4, 4, 32, 128)[:, :3]
+
+    sent.append(start(parts.at[1 - k], other, 18, 18, (s, chan[1])))
+    wait_in(other, 18)
+
+    @pl.loop(0, 3)
+    def _(b):
+        sums[b] = (
+            parts[k, b].astype(jnp.float32) + other[b].astype(jnp.float32)
+        ).astype(jnp.bfloat16)
+
+    def block(owner):
+        return sums.at[:, owner // 2, :, pl.ds(pl.multiple_of(16 * lax.rem(owner, 2), 16), 16)]
+
+    for step in range(1, spaces):
+        owner = lax.rem(s + step, spaces)
+        sent.append(start(block(owner), landed.at[step], 18 + step, 18 + step, (owner, c)))
+    own = pltpu.make_async_copy(block(s), landed.at[0], local.at[1])
+    own.start()
+
+    wait_in(place(1), 12)
+    wait_in(place(1), 13)
+    wait_in(place(1), 14)
+    for from_x in range(2):
+        wait_in(place(1), 15 + from_x)
+    for j in (1, 2, 3):
+        wait_in(wg.at[0], 8 + j)
+    stencil(lambda: jnp.concatenate([wg[j] for j in range(4)], axis=1), gp, total)
+
+    @pl.loop(0, rows)
+    def _(h):
+        part_gi = total[h].reshape(2, 32, 128).astype(jnp.bfloat16)
+        rolled[h, :, 0] = part_gi
+
+    sent.append(start(rolled.at[:, 1 - k, 0], gi_ref.at[:, k], 18 + spaces, 18 + spaces, (s, chan[1])))
+    copy_gi = pltpu.make_async_copy(rolled.at[:, k, 0], gi_ref.at[:, k], local.at[2])
+    copy_gi.start()
+
+    own.wait()
+    for step in range(1, spaces):
+        wait_in(landed.at[step], 18 + step)
+    whole = landed[0].astype(jnp.float32)
+    for step in range(1, spaces):
+        whole = whole + landed[step].astype(jnp.float32)
+    gw_ref[...] = whole
+
+    copy_out.wait()
+    copy_gi.wait()
+    wait_in(out_ref.at[:, 1 - k], 17)
+    wait_in(gi_ref.at[:, 1 - k], 18 + spaces)
+    for copy in sent:
+        copy.wait_send()
+
+
+def fused(inputs, weight, cotangent):
+    spaces = lax.axis_size("space")
+    count, planes, rows, cols = inputs.shape
+    taps = weight.reshape(4, 32, 3, 3, 3, 32)
+    wf = jnp.pad(
+        jnp.transpose(taps, (3, 4, 5, 0, 2, 1)), ((0, 0),) * 4 + ((0, 1), (0, 0))
+    ).reshape(288, 512)
+    flipped = taps[:, :, ::-1, ::-1, ::-1]
+    wg = jnp.pad(
+        jnp.transpose(flipped, (0, 3, 4, 1, 2, 5)), ((0, 0),) * 4 + ((0, 1), (0, 0))
+    ).reshape(2, 576, 128)
+    x, cot = (jnp.transpose(one, (2, 1, 0, 3)) for one in (inputs, cotangent))
+    bf, sems = jnp.bfloat16, 19 + spaces
+    vmem = pl.BlockSpec(memory_space=pltpu.VMEM)
+    out, gi, gw = pl.pallas_call(
+        functools.partial(kernel, spaces),
+        out_shape=(
+            jax.ShapeDtypeStruct((rows, planes, count, cols), bf),
+            jax.ShapeDtypeStruct((rows, planes, count, cols), bf),
+            jax.ShapeDtypeStruct((3, 3, 16, 128), jnp.float32),
+        ),
+        in_specs=[vmem] * 4,
+        out_specs=(vmem,) * 3,
+        scratch_shapes=[
+            pltpu.VMEM((rows, 4, 4, 32, cols), bf),
+            pltpu.VMEM((rows, 4, 4, 32, cols), bf),
+            pltpu.VMEM((2, 288, 512), bf),
+            pltpu.VMEM((4, 576, 128), bf),
+            pltpu.VMEM((rows, 2, 32, cols), bf),
+            pltpu.VMEM((rows, 2, 4, 32, cols), bf),
+            pltpu.VMEM((rows, 64, cols), jnp.float32),
+            pltpu.VMEM((2, 3, 4, 3, 32, 128), bf),
+            pltpu.VMEM((3, 4, 3, 32, 128), bf),
+            pltpu.VMEM((3, 4, 3, 32, 128), bf),
+            pltpu.VMEM((spaces, 3, 3, 16, 128), bf),
+            pltpu.VMEM((rows, 2, 32, cols), bf),
+            pltpu.SemaphoreType.DMA((sems,)),
+            pltpu.SemaphoreType.DMA((sems,)),
+            pltpu.SemaphoreType.DMA((4,)),
+        ],
+        compiler_params=pltpu.CompilerParams(
+            collective_id=0, has_side_effects=True, vmem_limit_bytes=48 * 1024 * 1024
+        ),
+    )(x, cot, wf, wg)
+    gw = jnp.transpose(gw.reshape(3, 3, 16, 4, 32)[:, :, :, :3], (2, 1, 0, 3, 4))
+    return (
+        jnp.transpose(out, (2, 1, 0, 3)),
+        jnp.transpose(gi, (2, 1, 0, 3)),
+        gw.reshape(16, 27, 32),
+    )
+
+
 def solution(mesh):
     in_specs = (
         P("chan", "space", None, None),
@@ -90,6 +333,12 @@
         P("chan", "space", None, None),
         P("space", None, "chan"),
     )
+
+    def body(inputs, weight, cotangent):
+        fits = inputs.shape[0] == 32 and inputs.shape[1] == 2 and inputs.shape[3] == 128
+        fits = fits and weight.shape == (128, 27, 32) and mesh.shape["space"] == 8
+        return (fused if fits else per_device)(inputs, weight, cotangent)
+
     return jax.shard_map(
-        per_device, mesh=mesh, in_specs=in_specs, out_specs=out_specs, check_vma=False
-    )
+        body, mesh=mesh, in_specs=in_specs, out_specs=out_specs, check_vma=False
+    )

time: 179 us -> 66.9 us (0.37)
  waiting for transfers between devices: 65.3 us -> 0 us
  Pallas kernels: 0 us -> 52.9 us
  matrix products: 41.6 us -> 0 us
  starting transfers between devices: 28.9 us -> 0 us
  between operations: 14.6 us -> 0.75 us
  blocking collectives: 9.91 us -> 0 us
  local copies, waits for them, and re-layouts: 16.5 us -> 13.1 us
    pallas_call x0 -> x1, Pallas kernels: none -> 52.9 us  [fused(): pl.pallas_call(functools.partial(kernel, spaces), out_shape=(jax.ShapeDty...]
    reduce_scatter x1 -> x0, waiting for transfers between devices: 44.5 us -> none  [per_device(): lax.psum_scatter(jnp.stack(tap_list, axis=1), 'space', scatter_dimension=...]
    dot_general x80 -> x0, matrix products: 41.3 us -> none  [the longest x27 24.1 us: per_device(): jnp.einsum('idhw,odhw->io', piece, grad_pre, preferred_element_type=jnp.f...]
    all_to_all x4 -> x0, starting transfers between devices: 15.1 us -> none  [the longest x1 4.21 us: per_device(): lax.all_to_all(inputs, 'chan', split_axis=2, concat_axis=0, tiled=True)]
    ppermute x8 -> x0, starting transfers between devices: 13.7 us -> none  [the longest x4 11.2 us: padded(): lax.ppermute(head, axis, [((i + 1) % count, i) for i in range(count)])]
    unnamed x14 -> x6, local copies, waits for them, and re-layouts: 11.8 us -> 1.76 us
    all_gather x1 -> x0, blocking collectives: 9.91 us -> none  [per_device(): filters = lax.all_gather(weight, 'chan', axis=2, tiled=True)]
    ppermute x8 -> x0, waiting for transfers between devices: 9.88 us -> none  [the longest x4 5.53 us: padded(): lax.ppermute(tail, axis, [(i, (i + 1) % count) for i in range(count)])]
  transfers between devices with their start and end apart: 14 -> 0, of which waited for: 10 -> 0; matrix products, arithmetic and copies ran while one was open for 15% -> 0% of each run, Pallas kernels for 0% -> 0%
where the time goes in v1:
time: 66.9 us; the launch traced here: 66.8 us
  Pallas kernels  52.9 us (79%)
  local copies, waits for them, and re-layouts  13.1 us (20%)
  between operations  0.75 us (1%)
    pallas_call x1, Pallas kernels, fused(): pl.pallas_call(functools.partial(kernel, spaces), out_shape=(jax.ShapeDty...  52.9 us
    reshape x3, local copies, waits for them, and re-layouts, fused(): taps = weight.reshape(4, 32, 3, 3, 3, 32)  4.1 us
    rev x1, local copies, waits for them, and re-layouts, fused(): flipped = taps[:, :, ::-1, ::-1, ::-1]  2.96 us
    unnamed x6, local copies, waits for them, and re-layouts  1.76 us

profile of v1, /device:TPU:0, one launch (start us, length us, event | category | flops | bytes accessed | tf_op | source)
XLA Modules:
  0.0 66.8 jit_solution(1441593966013061388)
XLA Ops:
  0.6 1.9 %reshape.21 = bf16[4,32,3,3,3,32]{1,0,5,4,3,2:T(4,128)(2,1)S(1)} reshape(bf16[128,27,32]{0,2,1:T(8,128)(2,1)} %param.4) | data formatting | bytes 442368 | tf_op jit(solution)/shard_map/reshape | solution.py:276
  2.6 1.0 %copy.9 = bf16[4,32,3,3,3,32]{5,2,1,4,3,0:T(4,128)(2,1)S(1)} copy(bf16[4,32,3,3,3,32]{1,0,5,4,3,2:T(4,128)(2,1)S(1)} %reshape.21) | data formatting | bytes 442368 | tf_op jit(solution)/shard_map/reshape | solution.py:276
  3.5 3.0 %rev.3 = bf16[4,32,3,3,3,32]{5,2,1,4,3,0:T(4,128)(2,1)S(1)} reverse(bf16[4,32,3,3,3,32]{5,2,1,4,3,0:T(4,128)(2,1)S(1)} %copy.9), dimensions={2,3,4} | reverse | bytes 442368 | tf_op jit(solution)/shard_map/rev | solution.py:280
  6.5 0.8 %pad.9 = bf16[4,3,3,32,4,32]{5,4,3,2,1,0:T(4,128)(2,1)S(1)} pad(bf16[4,3,3,32,3,32]{5,4,3,2,1,0:T(4,128)(2,1)S(1)} %bitcast.19, bf16[]{:T(256)} %constant.2.clone.1), padding=0_0x0_0x0_0x0_0x0_1x0_0 | pad | bytes 516098 | tf_op jit(solution)/shard_map/jit(_pad)/pad | solution.py:281
  7.3 0.6 reshape.23.wg_ref
  7.9 1.2 %copy.16 = bf16[4,32,3,3,3,32]{1,2,0,5,4,3:T(4,128)(2,1)S(1)} copy(bf16[4,32,3,3,3,32]{1,0,5,4,3,2:T(4,128)(2,1)S(1)} %reshape.21) | data formatting | bytes 442368 | tf_op jit(solution)/shard_map/reshape | solution.py:276
  9.2 0.6 pad.8
  9.8 0.0 copy-start
  9.8 0.0 copy-start.1
  9.8 1.1 %reshape.22.wf_ref = bf16[288,512]{1,0:T(8,128)(2,1)S(1)} reshape(bf16[3,3,32,4,4,32]{5,4,3,2,1,0:T(4,128)(2,1)S(1)} %pad.8) | data formatting | bytes 589824 | tf_op jit(solution)/shard_map/reshape | solution.py:279
  11.0 0.0 copy-done
  11.0 0.0 copy-done.1
  11.0 0.2 copy_bitcast_fusion.1
  11.2 52.9 %shard_map.58 = (bf16[16,2,32,128]{3,2,1,0:T(8,128)(2,1)S(1)}, bf16[16,2,32,128]{3,2,1,0:T(8,128)(2,1)S(1)}, f32[3,3,16,128]{3,2,1,0:T(8,128)S(1)}) custom-call(bf16[16,2,32,128]{3,2,1,0:T(8,128)(2,1)S(1)} %get-tuple-element.13.x_ref, bf16[16,2,32,128]{3,2,1,0:T(8,128)(2,1)S(1)} %get-tuple-element.12.cot_ref, bf16[288,512]{1,0:T(8,128)(2,1)S(1)} %reshape.22.wf_ref, ...), custom_call_target="tpu_custom_call" | custom-call | tf_op jit(solution)/shard_map/pallas_call | solution.py:287
  64.1 0.2 reshape.24
  64.3 0.7 %copy.10 = f32[16,3,3,3,32]{4,0,3,2,1:T(8,128)} copy(f32[16,3,3,3,32]{4,3,0,1,2:T(4,128)S(1)} %slice_bitcast_fusion) | data formatting | bytes 110592 | tf_op jit(solution)/shard_map/transpose | solution.py:317
  65.0 0.9 %copy.11 = bf16[32,2,16,128]{3,2,1,0:T(8,128)(2,1)} copy(bf16[32,2,16,128]{3,0,1,2:T(8,128)(2,1)S(1)} %bitcast.18) | data formatting | bytes 524288
  65.9 0.9 %copy.12 = bf16[32,2,16,128]{3,2,1,0:T(8,128)(2,1)} copy(bf16[32,2,16,128]{3,0,1,2:T(8,128)(2,1)S(1)} %bitcast.17) | data formatting | bytes 524288
  (1 shorter events, 0.0 us)
Async XLA Ops:
  9.8 1.2 %copy-start = (bf16[32,2,16,128]{3,2,1,0:T(8,128)(2,1)S(1)}, bf16[32,2,16,128]{3,2,1,0:T(8,128)(2,1)}, u32[]{:S(2)}) copy-start(bf16[32,2,16,128]{3,2,1,0:T(8,128)(2,1)} %param.5) | copy-start | bytes 786436
  9.8 1.2 %copy-start.1 = (bf16[32,2,16,128]{3,2,1,0:T(8,128)(2,1)S(1)}, bf16[32,2,16,128]{3,2,1,0:T(8,128)(2,1)}, u32[]{:S(2)}) copy-start(bf16[32,2,16,128]{3,2,1,0:T(8,128)(2,1)} %param.3) | copy-start | bytes 786436

commit v2 on v1

v2 whole, which is shorter than its diff:
```python
import functools

import jax
import jax.numpy as jnp
from jax import lax
from jax.experimental import pallas as pl
from jax.experimental.pallas import tpu as pltpu
from jax.sharding import PartitionSpec as P


def padded(cells, sides, width):
    for axis, dim in sides:
        count = lax.axis_size(axis)
        head = lax.slice_in_dim(cells, 0, width, axis=dim)
        tail = lax.slice_in_dim(cells, cells.shape[dim] - width, cells.shape[dim], axis=dim)
        cells = jnp.concatenate(
            [
                lax.ppermute(tail, axis, [(i, (i + 1) % count) for i in range(count)]),
                cells,
                lax.ppermute(head, axis, [((i + 1) % count, i) for i in range(count)]),
            ],
            axis=dim,
        )
    return cells


def tap_offsets():
    return [
        (shift_d, shift_h, shift_w)
        for shift_d in (-1, 0, 1)
        for shift_h in (-1, 0, 1)
        for shift_w in (-1, 0, 1)
    ]


def per_device(inputs, weight, cotangent):
    depth_local = inputs.shape[1]
    moved_inputs, moved_cot = (
        lax.all_to_all(inputs, "chan", split_axis=2, concat_axis=0, tiled=True),
        lax.all_to_all(cotangent, "chan", split_axis=2, concat_axis=0, tiled=True),
    )
    rows_local = moved_inputs.shape[2]
    extended = padded(moved_inputs, (("space", 1), ("chan", 2)), 1)
    filters = lax.all_gather(weight, "chan", axis=2, tiled=True)
    pre_act = jnp.zeros(moved_inputs.shape, jnp.float32)
    for index_tap, (shift_d, shift_h, shift_w) in enumerate(tap_offsets()):
        piece = extended[
            :, 1 + shift_d : 1 + shift_d + depth_local, 1 + shift_h : 1 + shift_h + rows_local
        ]
        piece = jnp.roll(piece, -shift_w, axis=3)
        pre_act = pre_act + jnp.einsum(
            "idhw,io->odhw", piece, filters[:, index_tap, :], preferred_element_type=jnp.float32
        )
    out_local = jnp.maximum(pre_act, 0.0).astype(jnp.bfloat16)
    grad_pre = jnp.where(pre_act > 0, moved_cot.astype(jnp.float32), 0.0).astype(jnp.bfloat16)
    output = lax.all_to_all(out_local, "chan", split_axis=0, concat_axis=2, tiled=True)
    grad_ext = padded(grad_pre, (("space", 1), ("chan", 2)), 1)
    grad_sum = jnp.zeros(moved_inputs.shape, jnp.float32)
    for index_tap, (shift_d, shift_h, shift_w) in enumerate(tap_offsets()):
        piece = grad_ext[
            :, 1 - shift_d : 1 - shift_d + depth_local, 1 - shift_h : 1 - shift_h + rows_local
        ]
        piece = jnp.roll(piece, shift_w, axis=3)
        grad_sum = grad_sum + jnp.einsum(
            "odhw,io->idhw", piece, filters[:, index_tap, :], preferred_element_type=jnp.float32
        )
    grad_inputs = lax.all_to_all(
        grad_sum.astype(jnp.bfloat16), "chan", split_axis=0, concat_axis=2, tiled=True
    )
    tap_list = []
    for index_tap, (shift_d, shift_h, shift_w) in enumerate(tap_offsets()):
        piece = extended[
            :, 1 + shift_d : 1 + shift_d + depth_local, 1 + shift_h : 1 + shift_h + rows_local
        ]
        piece = jnp.roll(piece, -shift_w, axis=3)
        tap_list.append(
            jnp.einsum("idhw,odhw->io", piece, grad_pre, preferred_element_type=jnp.float32)
        )
    partial_sum = lax.psum_scatter(
        jnp.stack(tap_list, axis=1), "space", scatter_dimension=0, tiled=True
    )
    grad_weight = lax.psum_scatter(partial_sum, "chan", scatter_dimension=2, tiled=True)
    return (output, grad_inputs, grad_weight)


MESH = pl.DeviceIdType.MESH
CHUNKS = 4


def stencil(filters, cells, total, first, last, sign):
    rows = total.shape[0]

    @pl.loop(first // 2, last // 2)
    def _(pair):
        right = jnp.concatenate(
            [cells[2 * pair + one].reshape(-1, 128) for one in range(2)], axis=1
        )
        terms = jnp.dot(filters(), right, preferred_element_type=jnp.float32)
        for half in range(2):
            part = terms[:, 128 * half : 128 * half + 128].reshape(3, 3, 64, 128)
            for b in range(3):
                row = lax.rem(2 * pair + half + rows - sign * (b - 1), rows)
                total[row] += (
                    part[b, 1]
                    + pltpu.roll(part[b, 1 - sign], 1, 1)
                    + pltpu.roll(part[b, 1 + sign], 127, 1)
                )


def kernel(
    spaces, x_ref, cot_ref, w_ref, out_ref, gi_ref, gw_ref,
    xg, gp, wf, wg, cot, rolled, total, back, parts, other, sums, landed, part_out,
    send, recv, local,
):
    s, c = lax.axis_index("space"), lax.axis_index("chan")
    x, k = c // 2, lax.rem(c, 2)
    chan = [c, 2 * x + 1 - k, lax.rem(c + 2, 4), 2 * (1 - x) + 1 - k]
    up, down = lax.rem(s + 1, spaces), lax.rem(s + spaces - 1, spaces)
    rows = x_ref.shape[0]
    chunks = CHUNKS
    tall = rows // chunks
    edges = [0] + [tall * q - 2 for q in range(1, chunks)] + [rows]
    base_gp, base = 7 * chunks, 12 * chunks

    barrier = pltpu.get_barrier_semaphore()
    greeted = [(s, other_c) for other_c in chan[1:]]
    greeted += [(side, other_c) for side in (up, down) for other_c in range(4)]
    greeted += [(lax.rem(s + step, spaces), c) for step in range(2, spaces - 1)]
    for device in greeted:
        pl.semaphore_signal(barrier, inc=1, device_id=device, device_id_type=MESH)
    pl.semaphore_wait(barrier, len(greeted))

    sent = []

    def start(src, dst, out_sem, in_sem, device):
        copy = pltpu.make_async_remote_copy(
            src_ref=src, dst_ref=dst, send_sem=send.at[out_sem], recv_sem=recv.at[in_sem],
            device_id=device, device_id_type=MESH,
        )
        copy.start()
        sent.append(copy)

    def wait_in(dst, in_sem):
        pltpu.make_async_copy(dst, dst, recv.at[in_sem]).wait()

    def span(q):
        return pl.ds(tall * q, tall)

    keep = [
        pltpu.make_async_copy(x_ref, xg.at[:, pl.ds(1 - k, 2), c], local.at[0]),
        pltpu.make_async_copy(cot_ref.at[:, k], cot.at[:, k], local.at[1]),
        pltpu.make_async_copy(w_ref.at[:, pl.ds(pl.multiple_of(64 * x, 64), 64)], wg.at[c], local.at[2]),
    ]
    for copy in keep:
        copy.start()
    for q in range(chunks):
        at, mine = 7 * q, x_ref.at[span(q)]
        start(mine, xg.at[span(q), pl.ds(1 - k, 2), c], at + 1, at + 1, (s, chan[2]))
        for plane, side in ((0, down), (1, up)):
            for to_x in range(2):
                start(
                    x_ref.at[span(q), plane], xg.at[span(q), 2 * (1 - plane), c],
                    at + 3 + 2 * plane + to_x, at + 3 + c, (side, 2 * to_x + 1 - plane),
                )
        start(mine, xg.at[span(q), pl.ds(k, 2), c], at, at, (s, chan[1]))
    start(cot_ref.at[:, 1 - k], cot.at[:, k], base, base, (s, chan[1]))

    for tap in range(9):
        turned = jnp.transpose(w_ref[tap].astype(jnp.float32)).astype(jnp.bfloat16)
        for a in range(3):
            wf[tap, k, :, 128 * a : 128 * a + 128] = turned[32 * a : 32 * a + 32]
    start(wf.at[:, k], wf.at[:, k], base + 1, base + 1, (s, chan[1]))
    for j in (2, 3, 1):
        half = pl.ds(pl.multiple_of(64 * (chan[j] // 2), 64), 64)
        start(w_ref.at[:, half], wg.at[c], base + 1 + j, base + 1 + j, (s, chan[j]))

    zero = jnp.zeros((4, 32, 128), jnp.bfloat16)

    @pl.loop(0, rows)
    def _(h):
        gp[h, :, 3] = zero
        rolled[h, :, 3] = zero[:2]
        total[h] = jnp.zeros((64, 128), jnp.float32)
        back[h] = jnp.zeros((64, 128), jnp.float32)

    def segment(q):
        return pl.ds(edges[q], edges[q + 1] - edges[q])

    def place(q, slot, of_x=x):
        return gp.at[segment(q), pl.ds(2 * of_x, 2), slot]

    side = lax.rem(s + spaces + 2 * k - 1, spaces)

    for copy in keep:
        copy.wait()
    for q in range(chunks):
        at = 7 * q
        came = xg.at[span(q), pl.ds(1 - k, 2), chan[2]]
        wait_in(came, at + 1)
        start(came, xg.at[span(q), pl.ds(k, 2), chan[2]], at + 2, at + 2, (s, chan[1]))
        wait_in(xg.at[span(q), pl.ds(1 - k, 2), chan[1]], at)
        for from_c in range(4):
            wait_in(xg.at[span(q), 2 * k, from_c], at + 3 + from_c)
        wait_in(xg.at[span(q), pl.ds(1 - k, 2), chan[3]], at + 2)
        if q == 0:
            wait_in(wf.at[:, 1 - k], base + 1)
        stencil(lambda: wf[...].reshape(576, 384), xg, total, tall * q, tall * q + tall, 1)
        if q == 0:
            wait_in(cot.at[:, 1 - k], base)

        @pl.loop(edges[q], edges[q + 1])
        def _(r):
            h = lax.rem(r + 1, rows)
            pre = total[h].reshape(2, 32, 128)
            part_out[h] = jnp.maximum(pre, 0.0).astype(jnp.bfloat16)
            grad = jnp.where(pre > 0, cot[h].astype(jnp.float32), 0.0)
            gp[r, pl.ds(2 * x, 2), 1] = grad.astype(jnp.bfloat16)
            flat = grad.reshape(64, 128)
            rolled[h, :, 0] = pltpu.roll(flat, 127, 1).reshape(2, 32, 128).astype(jnp.bfloat16)
            rolled[h, :, 1] = grad.astype(jnp.bfloat16)
            rolled[h, :, 2] = pltpu.roll(flat, 1, 1).reshape(2, 32, 128).astype(jnp.bfloat16)

        at = base_gp + 5 * q
        start(place(q, 1), place(q, 1), at + 1, at + 1, (s, chan[2]))
        for to_x in range(2):
            start(place(q, 1), place(q, 2 * k), at + 3 + to_x, at + 3 + x, (side, 2 * to_x + 1 - k))
        start(place(q, 1), place(q, 2 * (1 - k)), at, at, (s, chan[1]))

    start(part_out.at[:, 1 - k], out_ref.at[:, k], base + 5, base + 5, (s, chan[1]))
    copy_out = pltpu.make_async_copy(part_out.at[:, k], out_ref.at[:, k], local.at[0])
    copy_out.start()

    def relay(q):
        at = base_gp + 5 * q
        came = place(q, 1, 1 - x)
        wait_in(came, at + 1)
        start(came, place(q, 2 * (1 - k), 1 - x), at + 2, at + 2, (s, chan[1]))

    def filter_sums(b):
        left = jnp.concatenate(
            [xg[(h + b - 1) % rows].reshape(384, 128) for h in range(rows)], axis=1
        )
        right = jnp.concatenate([rolled[h].reshape(256, 128) for h in range(rows)], axis=1)
        got = lax.dot_general(
            left, right, (((1,), (1,)), ((), ())), preferred_element_type=jnp.float32
        ).astype(jnp.bfloat16)
        for half in range(2):
            parts[half, b] = got[:, 128 * half : 128 * half + 128].reshape(3, 128, 128)

    for q in range(chunks - 2):
        relay(q)
    filter_sums(0)
    relay(chunks - 2)
    filter_sums(1)
    filter_sums(2)
    start(parts.at[1 - k], other, base + 6, base + 6, (s, chan[1]))
    relay(chunks - 1)
    wait_in(other, base + 6)

    @pl.loop(0, 3)
    def _(b):
        sums[b] = (
            parts[k, b].astype(jnp.float32) + other[b].astype(jnp.float32)
        ).astype(jnp.bfloat16)

    def block(owner):
        return sums.at[:, :, pl.ds(pl.multiple_of(16 * owner, 16), 16)]

    for step in range(1, spaces):
        owner = lax.rem(s + step, spaces)
        start(block(owner), landed.at[step], base + 6 + step, base + 6 + step, (owner, c))
    own = pltpu.make_async_copy(block(s), landed.at[0], local.at[1])
    own.start()

    for j in (1, 2, 3):
        wait_in(wg.at[chan[j]], base + 1 + j)
    for q in range(chunks):
        at = base_gp + 5 * q
        wait_in(place(q, 2 * k), at)
        wait_in(place(q, 2 * k, 1 - x), at + 2)
        for from_x in range(2):
            wait_in(place(q, 2 * (1 - k), from_x), at + 3 + from_x)
        stencil(
            lambda: jnp.concatenate([wg[j].reshape(576, 128) for j in range(4)], axis=1),
            gp, back, edges[q], edges[q + 1], -1,
        )

    @pl.loop(0, rows)
    def _(r):
        rolled[lax.rem(r + 1, rows), :, 0] = back[r].reshape(2, 32, 128).astype(jnp.bfloat16)

    last = base + 6 + spaces
    start(rolled.at[:, 1 - k, 0], gi_ref.at[:, k], last, last, (s, chan[1]))
    copy_gi = pltpu.make_async_copy(rolled.at[:, k, 0], gi_ref.at[:, k], local.at[2])
    copy_gi.start()

    own.wait()
    for step in range(1, spaces):
        wait_in(landed.at[step], base + 6 + step)
    whole = landed[0].astype(jnp.float32)
    for step in range(1, spaces):
        whole = whole + landed[step].astype(jnp.float32)
    gw_ref[...] = whole

    copy_out.wait()
    copy_gi.wait()
    wait_in(out_ref.at[:, 1 - k], base + 5)
    wait_in(gi_ref.at[:, 1 - k], last)
    for copy in sent:
        copy.wait_send()


def fused(inputs, weight, cotangent):
    spaces = lax.axis_size("space")
    count, planes, rows, cols = inputs.shape
    bf, sems = jnp.bfloat16, 12 * CHUNKS + 7 + spaces
    taps = jnp.transpose(weight, (1, 0, 2)).reshape(3, 9, 128, 32)
    filters = jnp.concatenate([taps[0], taps[1], taps[2], jnp.zeros_like(taps[0])], axis=2)
    x, cot = (jnp.transpose(one, (2, 1, 0, 3)) for one in (inputs, cotangent))
    vmem = pl.BlockSpec(memory_space=pltpu.VMEM)
    out, gi, gw = pl.pallas_call(
        functools.partial(kernel, spaces),
        out_shape=(
            jax.ShapeDtypeStruct((rows, planes, count, cols), bf),
            jax.ShapeDtypeStruct((rows, planes, count, cols), bf),
            jax.ShapeDtypeStruct((3, 3, 16, 128), jnp.float32),
        ),
        in_specs=[vmem] * 3,
        out_specs=(vmem,) * 3,
        scratch_shapes=[
            pltpu.VMEM((rows, 3, 4, 32, cols), bf),
            pltpu.VMEM((rows, 4, 4, 32, cols), bf),
            pltpu.VMEM((9, 2, 32, 384), bf),
            pltpu.VMEM((4, 9, 64, 128), bf),
            pltpu.VMEM((rows, 2, 32, cols), bf),
            pltpu.VMEM((rows, 2, 4, 32, cols), bf),
            pltpu.VMEM((rows, 64, cols), jnp.float32),
            pltpu.VMEM((rows, 64, cols), jnp.float32),
            pltpu.VMEM((2, 3, 3, 128, 128), bf),
            pltpu.VMEM((3, 3, 128, 128), bf),
            pltpu.VMEM((3, 3, 128, 128), bf),
            pltpu.VMEM((spaces, 3, 3, 16, 128), bf),
            pltpu.VMEM((rows, 2, 32, cols), bf),
            pltpu.SemaphoreType.DMA((sems,)),
            pltpu.SemaphoreType.DMA((sems,)),
            pltpu.SemaphoreType.DMA((3,)),
        ],
        compiler_params=pltpu.CompilerParams(
            collective_id=0, has_side_effects=True, vmem_limit_bytes=48 * 1024 * 1024
        ),
    )(x, cot, filters)
    gw = jnp.transpose(gw.reshape(3, 3, 16, 4, 32)[:, :, :, :3], (2, 1, 0, 3, 4))
    return (
        jnp.transpose(out, (2, 1, 0, 3)),
        jnp.transpose(gi, (2, 1, 0, 3)),
        gw.reshape(16, 27, 32),
    )


def solution(mesh):
    in_specs = (
        P("chan", "space", None, None),
        P(None, None, "chan"),
        P("chan", "space", None, None),
    )
    out_specs = (
        P("chan", "space", None, None),
        P("chan", "space", None, None),
        P("space", None, "chan"),
    )

    def body(inputs, weight, cotangent):
        fits = inputs.shape[0] == 32 and inputs.shape[1] == 2 and inputs.shape[3] == 128
        fits = fits and weight.shape == (128, 27, 32) and mesh.shape["space"] == 8
        return (fused if fits else per_device)(inputs, weight, cotangent)

    return jax.shard_map(
        body, mesh=mesh, in_specs=in_specs, out_specs=out_specs, check_vma=False
    )
```

time: 66.9 us -> 50 us (0.75)
  Pallas kernels: 52.9 us -> 43.4 us
  local copies, waits for them, and re-layouts: 13.1 us -> 5.08 us
    pallas_call x1, Pallas kernels: 52.9 us -> 43.4 us  [fused(): pl.pallas_call(functools.partial(kernel, spaces), out_shape=(jax.ShapeDty...]
    reshape x5 -> x0, local copies, waits for them, and re-layouts: 5.81 us -> none  [the longest x3 4.1 us: fused(): taps = weight.reshape(4, 32, 3, 3, 3, 32)]
    rev x1 -> x0, local copies, waits for them, and re-layouts: 2.96 us -> none  [fused(): flipped = taps[:, :, ::-1, ::-1, ::-1]]
    unnamed x6 -> x7, local copies, waits for them, and re-layouts: 1.76 us -> 3.84 us
    pad x2 -> x0, local copies, waits for them, and re-layouts: 1.47 us -> none  [the longest x1 0.83 us: fused(): jnp.pad(jnp.transpose(flipped, (0, 3, 4, 1, 2, 5)), ((0, 0),) * 4 + ((0,...]
where the time goes in v2:
time: 50 us; the launch traced here: 49.5 us
  Pallas kernels  43.4 us (87%)
  local copies, waits for them, and re-layouts  5.08 us (10%)
  between operations  0.68 us (1%)
    pallas_call x1, Pallas kernels, fused(): pl.pallas_call(functools.partial(kernel, spaces), out_shape=(jax.ShapeDty...  43.4 us
    unnamed x7, local copies, waits for them, and re-layouts  3.84 us

profile of v2, /device:TPU:0, one launch (start us, length us, event | category | flops | bytes accessed | tf_op | source)
XLA Modules:
  0.0 49.5 jit_solution(14053537826294287546)
XLA Ops:
  0.6 1.4 %copy.8 = bf16[128,27,32]{2,0,1:T(8,128)(2,1)S(1)} copy(bf16[128,27,32]{0,2,1:T(8,128)(2,1)} %param.4) | data formatting | bytes 442368 | tf_op args[1]
  2.0 0.1 fusion
  2.1 0.1 pad.3.clone
  2.1 0.0 copy-start
  2.1 0.0 copy-start.1
  2.1 0.3 maximum_maximum_fusion.w_ref
  2.4 0.7 %copy-done = bf16[32,2,16,128]{3,2,1,0:T(8,128)(2,1)S(1)} copy-done((bf16[32,2,16,128]{3,2,1,0:T(8,128)(2,1)S(1)}, bf16[32,2,16,128]{3,2,1,0:T(8,128)(2,1)}, u32[]{:S(2)}) %copy-start) | copy-done | bytes 262168
  3.1 0.1 copy-done.1
  3.2 0.2 copy_bitcast_fusion
  3.4 43.4 %shard_map.58 = (bf16[16,2,32,128]{3,2,1,0:T(8,128)(2,1)S(1)}, bf16[16,2,32,128]{3,2,1,0:T(8,128)(2,1)S(1)}, f32[3,3,16,128]{3,2,1,0:T(8,128)S(1)}) custom-call(bf16[16,2,32,128]{3,2,1,0:T(8,128)(2,1)S(1)} %get-tuple-element.16.x_ref, bf16[16,2,32,128]{3,2,1,0:T(8,128)(2,1)S(1)} %get-tuple-element.15.cot_ref, bf16[9,128,128]{2,1,0:T(8,128)(2,1)S(1)} %maximum_maximum_fusion.w_ref), custom_call_target="tpu_custom_call" | custom-call | tf_op jit(solution)/shard_map/pallas_call | solution.py:321
  46.8 0.2 reshape.19
  47.0 0.7 %copy.9 = f32[16,3,3,3,32]{4,0,3,2,1:T(8,128)} copy(f32[16,3,3,3,32]{4,3,0,1,2:T(4,128)S(1)} %slice_bitcast_fusion) | data formatting | bytes 110592 | tf_op jit(solution)/shard_map/transpose | solution.py:352
  47.7 0.9 %copy.10 = bf16[32,2,16,128]{3,2,1,0:T(8,128)(2,1)} copy(bf16[32,2,16,128]{3,0,1,2:T(8,128)(2,1)S(1)} %bitcast.13) | data formatting | bytes 524288
  48.6 0.9 %copy.11 = bf16[32,2,16,128]{3,2,1,0:T(8,128)(2,1)} copy(bf16[32,2,16,128]{3,0,1,2:T(8,128)(2,1)S(1)} %bitcast.12) | data formatting | bytes 524288
  (2 shorter events, 0.0 us)
Async XLA Ops:
  2.1 1.0 %copy-start = (bf16[32,2,16,128]{3,2,1,0:T(8,128)(2,1)S(1)}, bf16[32,2,16,128]{3,2,1,0:T(8,128)(2,1)}, u32[]{:S(2)}) copy-start(bf16[32,2,16,128]{3,2,1,0:T(8,128)(2,1)} %param.5) | copy-start | bytes 786436
  2.1 1.0 %copy-start.1 = (bf16[32,2,16,128]{3,2,1,0:T(8,128)(2,1)S(1)}, bf16[32,2,16,128]{3,2,1,0:T(8,128)(2,1)}, u32[]{:S(2)}) copy-start(bf16[32,2,16,128]{3,2,1,0:T(8,128)(2,1)} %param.3) | copy-start | bytes 786436

commit v3 on v2

--- a/solution.py
+++ b/solution.py
@@ -84,7 +84,7 @@
 
 
 MESH = pl.DeviceIdType.MESH
-CHUNKS = 4
+CHUNKS = 2
 
 
 def stencil(filters, cells, total, first, last, sign):
@@ -170,7 +170,7 @@
         for a in range(3):
             wf[tap, k, :, 128 * a : 128 * a + 128] = turned[32 * a : 32 * a + 32]
     start(wf.at[:, k], wf.at[:, k], base + 1, base + 1, (s, chan[1]))
-    for j in (2, 3, 1):
+    for j in (1, 2):
         half = pl.ds(pl.multiple_of(64 * (chan[j] // 2), 64), 64)
         start(w_ref.at[:, half], wg.at[c], base + 1 + j, base + 1 + j, (s, chan[j]))
 
@@ -247,6 +247,8 @@
         for half in range(2):
             parts[half, b] = got[:, 128 * half : 128 * half + 128].reshape(3, 128, 128)
 
+    wait_in(wg.at[chan[2]], base + 3)
+    start(wg.at[chan[2]], wg.at[chan[2]], base + 4, base + 4, (s, chan[1]))
     for q in range(chunks - 2):
         relay(q)
     filter_sums(0)
@@ -272,7 +274,7 @@
     own = pltpu.make_async_copy(block(s), landed.at[0], local.at[1])
     own.start()
 
-    for j in (1, 2, 3):
+    for j in (1, 3):
         wait_in(wg.at[chan[j]], base + 1 + j)
     for q in range(chunks):
         at = base_gp + 5 * q

time: 50 us -> 46.7 us (0.934)
  Pallas kernels: 43.4 us -> 40 us
    pallas_call x1, Pallas kernels: 43.4 us -> 40 us  [fused(): pl.pallas_call(functools.partial(kernel, spaces), out_shape=(jax.ShapeDty...]
where the time goes in v3:
time: 46.7 us; the launch traced here: 46.1 us
  Pallas kernels  40 us (86%)
  local copies, waits for them, and re-layouts  5.08 us (11%)
  between operations  0.68 us (1%)
    pallas_call x1, Pallas kernels, fused(): pl.pallas_call(functools.partial(kernel, spaces), out_shape=(jax.ShapeDty...  40 us
    unnamed x7, local copies, waits for them, and re-layouts  3.84 us

profile of v3, /device:TPU:0, one launch (start us, length us, event | category | flops | bytes accessed | tf_op | source)
XLA Modules:
  0.0 46.1 jit_solution(4806902996280031418)
XLA Ops:
  0.6 1.4 %copy.8 = bf16[128,27,32]{2,0,1:T(8,128)(2,1)S(1)} copy(bf16[128,27,32]{0,2,1:T(8,128)(2,1)} %param.4) | data formatting | bytes 442368 | tf_op args[1]
  2.0 0.1 fusion
  2.1 0.1 pad.3.clone
  2.1 0.0 copy-start
  2.1 0.0 copy-start.1
  2.1 0.3 maximum_maximum_fusion.w_ref
  2.4 0.7 %copy-done = bf16[32,2,16,128]{3,2,1,0:T(8,128)(2,1)S(1)} copy-done((bf16[32,2,16,128]{3,2,1,0:T(8,128)(2,1)S(1)}, bf16[32,2,16,128]{3,2,1,0:T(8,128)(2,1)}, u32[]{:S(2)}) %copy-start) | copy-done | bytes 262168
  3.1 0.1 copy-done.1
  3.2 0.2 copy_bitcast_fusion
  3.4 40.0 %shard_map.58 = (bf16[16,2,32,128]{3,2,1,0:T(8,128)(2,1)S(1)}, bf16[16,2,32,128]{3,2,1,0:T(8,128)(2,1)S(1)}, f32[3,3,16,128]{3,2,1,0:T(8,128)S(1)}) custom-call(bf16[16,2,32,128]{3,2,1,0:T(8,128)(2,1)S(1)} %get-tuple-element.16.x_ref, bf16[16,2,32,128]{3,2,1,0:T(8,128)(2,1)S(1)} %get-tuple-element.15.cot_ref, bf16[9,128,128]{2,1,0:T(8,128)(2,1)S(1)} %maximum_maximum_fusion.w_ref), custom_call_target="tpu_custom_call" | custom-call | tf_op jit(solution)/shard_map/pallas_call | solution.py:323
  43.4 0.2 reshape.19
  43.6 0.7 %copy.9 = f32[16,3,3,3,32]{4,0,3,2,1:T(8,128)} copy(f32[16,3,3,3,32]{4,3,0,1,2:T(4,128)S(1)} %slice_bitcast_fusion) | data formatting | bytes 110592 | tf_op jit(solution)/shard_map/transpose | solution.py:354
  44.3 0.9 %copy.10 = bf16[32,2,16,128]{3,2,1,0:T(8,128)(2,1)} copy(bf16[32,2,16,128]{3,0,1,2:T(8,128)(2,1)S(1)} %bitcast.13) | data formatting | bytes 524288
  45.2 0.9 %copy.11 = bf16[32,2,16,128]{3,2,1,0:T(8,128)(2,1)} copy(bf16[32,2,16,128]{3,0,1,2:T(8,128)(2,1)S(1)} %bitcast.12) | data formatting | bytes 524288
  (2 shorter events, 0.0 us)
Async XLA Ops:
  2.1 1.0 %copy-start = (bf16[32,2,16,128]{3,2,1,0:T(8,128)(2,1)S(1)}, bf16[32,2,16,128]{3,2,1,0:T(8,128)(2,1)}, u32[]{:S(2)}) copy-start(bf16[32,2,16,128]{3,2,1,0:T(8,128)(2,1)} %param.5) | copy-start | bytes 786436
  2.1 1.0 %copy-start.1 = (bf16[32,2,16,128]{3,2,1,0:T(8,128)(2,1)S(1)}, bf16[32,2,16,128]{3,2,1,0:T(8,128)(2,1)}, u32[]{:S(2)}) copy-start(bf16[32,2,16,128]{3,2,1,0:T(8,128)(2,1)} %param.3) | copy-start | bytes 786436
